TPU v7x, 32 devices: a whole 2x2x4 slice. The times are simulated.
32 devices in a mesh: tiles: 32 (over z, y, x, core).
Axes of the slice: x: 2, y: 2, z: 4, core: 2. Of those that a mesh axis runs over, the one named last changes fastest.
Arguments:
- primal_start: float32 [64, 512, 1024], P('tiles'), may hold values from 0 to 1
- cost: bfloat16 [64, 512, 1024], P('tiles'), may hold values from -4 to 4
- mask: int32 [64, 64, 8], P('tiles'), may hold values 0 or 1
- tile_adv: int32 [64], P('tiles'), may hold values from -1 to 31, as said below
- tile_slot: int32 [64], P('tiles'), may hold values from -1 to 31
- adv_dual: float32 [32, 512], P('tiles'), may hold values from 0 to 2
- slot_dual: float32 [32, 1024], P('tiles'), may hold values from 0 to 2
- spend_limit: float32 [32, 512], P('tiles'), may hold values from 204 to 921
- capacity: float32 [32, 1024], P('tiles'), may hold values from 64 to 384
Outputs:
- primal: float32 [64, 512, 1024], P('tiles')
- adv_out: float32 [32, 512], P('tiles')
- slot_out: float32 [32, 1024], P('tiles')
Inputs may be any that keep to these rules, and one draw needn't show every extreme that they name: -1 marks an empty tile slot; tile_adv and tile_slot are -1 at the same slots. Each device's 2 slots hold 1 to 2 tiles, in its first slots, and some device holds exactly 2.
All inputs are finite; a program needn't handle non-finite values. No bound on the sum of `mask` on one device may be relied on, other than what follows from the above.
Results may differ from a plain program's by a relative error of at most 0.0003.
Values sent between devices are 32-bit elements; how exact they have to be, the bound alone decides.
A program may use at most 64 MiB of HBM per device.

v0:
```python
import jax
import jax.numpy as jnp
from jax import lax
from jax.sharding import PartitionSpec as P

MB_ROWS = 8
MB_COLS = 128
ITERS = 2


tau_step = 0.5


def expand_mask(blocks, block_rows, block_cols):
    values = blocks.astype(jnp.float32)
    rows_in = values.shape[-2]
    cols_in = values.shape[-1]
    shaped = jnp.broadcast_to(
        values[..., :, None, :, None],
        values.shape[:-2] + (rows_in, block_rows, cols_in, block_cols),
    )
    return shaped.reshape(values.shape[:-2] + (rows_in * block_rows, cols_in * block_cols))


def body(primal_start, cost, mask, tile_adv, tile_slot, adv_dual, slot_dual, spend_limit, capacity):
    highest = lax.Precision.HIGHEST
    devices = lax.axis_size("tiles")
    adv_local = adv_dual.shape[0]
    slot_local = slot_dual.shape[0]
    rows_tile = primal_start.shape[1]
    cols_tile = primal_start.shape[2]
    adv_onehot = (
        tile_adv[:, None] == jnp.arange(adv_local * devices, dtype=jnp.int32)[None, :]
    ).astype(jnp.float32)
    slot_onehot = (
        tile_slot[:, None] == jnp.arange(slot_local * devices, dtype=jnp.int32)[None, :]
    ).astype(jnp.float32)
    present = (tile_adv >= 0).astype(jnp.float32)
    weight = expand_mask(mask, MB_ROWS, MB_COLS) * present[:, None, None]
    primal = weight * primal_start
    adv_all, slot_all, limit_all, capacity_all = (
        lax.all_gather(adv_dual, "tiles", axis=0, tiled=True),
        lax.all_gather(slot_dual, "tiles", axis=0, tiled=True),
        lax.all_gather(spend_limit, "tiles", axis=0, tiled=True),
        lax.all_gather(capacity, "tiles", axis=0, tiled=True),
    )
    for sweep_index in range(ITERS):
        adv_rows = jnp.dot(adv_onehot, adv_all, precision=highest)
        slot_cols = jnp.dot(slot_onehot, slot_all, precision=highest)
        update = weight * jnp.clip(
            primal
            - tau_step * (cost.astype(jnp.float32) + adv_rows[:, :, None] + slot_cols[:, None, :]),
            0.0,
            1.0,
        )
        extended = 2.0 * update - primal
        row_blocks = jnp.dot(adv_onehot.T, jnp.sum(extended, axis=2), precision=highest)
        col_blocks = jnp.dot(slot_onehot.T, jnp.sum(extended, axis=1), precision=highest)
        primal, row_blocks, col_blocks = (update, row_blocks, col_blocks)
        row_total, col_total = lax.psum((row_blocks, col_blocks), "tiles")
        adv_all = jnp.maximum(adv_all + (row_total - limit_all) / cols_tile, 0.0)
        slot_all = jnp.maximum(slot_all + (col_total - capacity_all) / rows_tile, 0.0)
    position = lax.axis_index("tiles")
    adv_dual = lax.dynamic_slice_in_dim(adv_all, position * adv_local, adv_local, 0)
    slot_dual = lax.dynamic_slice_in_dim(slot_all, position * slot_local, slot_local, 0)
    return (primal, adv_dual, slot_dual)


def solution(mesh):
    return jax.shard_map(
        body,
        mesh=mesh,
        in_specs=(
            P("tiles", None, None),
            P("tiles", None, None),
            P("tiles", None, None),
            P("tiles"),
            P("tiles"),
            P("tiles", None),
            P("tiles", None),
            P("tiles", None),
            P("tiles", None),
        ),
        out_specs=(P("tiles", None, None), P("tiles", None), P("tiles", None)),
        check_vma=False,
    )
```

profile of v0, /device:TPU:0, one launch (start us, length us, event | category | flops | bytes accessed | tf_op | source)
XLA Modules:
  0.0 363.4 jit_solution(6917808355549932551)
XLA Ops:
  7.2 0.0 copy-start.2
  7.2 0.0 copy-start.1
  7.2 0.0 copy-start.4
  7.2 0.0 copy-start.3
  7.2 0.0 all-reduce.7.cloned.1.call-start
  7.3 43.8 %all-gather.1 = f32[32,1,1024]{2,1,0:T(1,128)S(1)} all-gather(f32[1,1,1024]{2,1,0:T(1,128)} %bitcast.61), channel_id=1, replica_groups=mesh['tiles'=32] {'tiles'}, dimensions={0}, use_global_device_ids=true | all-gather | bytes 135168 | tf_op jit(solution)/shard_map/all_gather | solution.py:43
  51.1 0.0 copy-start
  51.1 37.2 %all-gather = f32[32,1,512]{2,1,0:T(1,128)S(1)} all-gather(f32[1,1,512]{2,1,0:T(1,128)} %bitcast.63), channel_id=1, replica_groups=mesh['tiles'=32] {'tiles'}, dimensions={0}, use_global_device_ids=true | all-gather | bytes 67584 | tf_op jit(solution)/shard_map/all_gather | solution.py:42
  88.3 0.7 compare_convert_fusion
  88.9 0.8 fusion.19
  89.8 0.7 convert_element_type.12
  90.5 0.1 copy.13
  90.6 0.9 fusion.13
  91.4 4.8 %fusion.18 = (f32[2,512]{1,0:T(2,128)S(1)}, f32[2,1024]{1,0:T(2,128)S(1)}) fusion(f32[2,512,1024]{2,1,0:T(8,128)} %param.9, f32[2]{0:T(128)S(1)} %compare_convert_fusion, f32[2,64,8]{2,1,0:T(8,128)S(1)} %copy.13, f32[2,1024]{1,0:T(2,128)S(1)} %fusion.13, f32[2,512]{1,0:T(2,128)S(1)} %fusion.19, bf16[2,512,1024]{2,1,0:T(8,128)(2,1)} %param.10), kind=kLoop, calls=%fused_computation.25 | loop fusion | flops 13628416 | bytes 6320136 | tf_op jit(solution)/shard_map/reduce_sum | solution.py:57
  96.2 0.0 copy-done.1
  96.2 1.0 fusion.29
  97.2 0.0 copy-done.2
  97.2 0.9 fusion.32
  98.1 0.0 all-reduce.7.cloned.1.call-update
  98.1 0.0 all-reduce.5.cloned.1.call-start
  98.2 0.0 copy-done.4
  98.2 38.1 %all-gather.2 = f32[32,1,512]{2,1,0:T(1,128)S(1)} all-gather(f32[1,1,512]{2,1,0:T(1,128)S(1)} %bitcast.64), channel_id=1, replica_groups=mesh['tiles'=32] {'tiles'}, dimensions={0}, use_global_device_ids=true | all-gather | bytes 67584 | tf_op jit(solution)/shard_map/all_gather | solution.py:44
  136.3 0.0 copy-done.3
  136.3 37.0 %all-gather.3 = f32[32,1,1024]{2,1,0:T(1,128)S(1)} all-gather(f32[1,1,1024]{2,1,0:T(1,128)S(1)} %bitcast.62), channel_id=1, replica_groups=mesh['tiles'=32] {'tiles'}, dimensions={0}, use_global_device_ids=true | all-gather | bytes 135168 | tf_op jit(solution)/shard_map/all_gather | solution.py:45
  173.3 45.7 %all-reduce.7.cloned.1.call-done = (f32[32,1024]{1,0:T(8,128)}, f32[32,512]{1,0:T(8,128)}) async-done(((f32[32,1024]{1,0:T(8,128)}, f32[32,512]{1,0:T(8,128)}), (f32[32,1024]{1,0:T(8,128)}, f32[32,512]{1,0:T(8,128)})) %all-reduce.7.cloned.1.call-update) | async-done | bytes 196624 | tf_op jit(solution)/shard_map/psum | solution.py:60
  219.0 1.0 fusion.15
  220.0 0.2 fusion.28
  220.2 0.9 fusion.21
  221.0 0.2 fusion.31
  221.2 0.0 copy-done
  221.2 6.4 %fusion.11 = (f32[2,1024]{1,0:T(2,128)S(1)}, f32[2,512]{1,0:T(2,128)S(1)}, f32[2,512,1024]{2,1,0:T(8,128)}) fusion(f32[2,1024]{1,0:T(2,128)S(1)} %fusion.13, f32[2,512]{1,0:T(2,128)S(1)} %fusion.19, bf16[2,512,1024]{2,1,0:T(8,128)(2,1)S(1)} %copy-done, f32[2,512,1024]{2,1,0:T(8,128)} %param.9, f32[2]{0:T(128)S(1)} %compare_convert_fusion, ...), kind=kLoop, calls=%fused_computation.16 | loop fusion | flops 19919872 | bytes 10526728 | tf_op jit(solution)/shard_map/reduce_sum | solution.py:58
  227.6 1.0 fusion.27
  228.6 0.9 fusion.30
  229.5 0.0 all-reduce.5.cloned.1.call-update
  229.6 124.3 %all-reduce.5.cloned.1.call-done = (f32[32,512]{1,0:T(8,128)}, f32[32,1024]{1,0:T(8,128)}) async-done(((f32[32,512]{1,0:T(8,128)}, f32[32,1024]{1,0:T(8,128)}), (f32[32,512]{1,0:T(8,128)}, f32[32,1024]{1,0:T(8,128)})) %all-reduce.5.cloned.1.call-update) | async-done | bytes 196624 | tf_op jit(solution)/shard_map/psum | solution.py:60
  353.9 1.4 fusion.23
  355.2 1.3 fusion.25
  (2 shorter events, 0.0 us)
Async XLA Ops:
  7.2 90.0 %copy-start.2 = (s32[2]{0:T(128)S(1)}, s32[2]{0:T(128)}, u32[]{:S(2)}) copy-start(s32[2]{0:T(128)} %param.12) | copy-start | bytes 28
  7.2 89.0 %copy-start.1 = (s32[2]{0:T(128)S(1)}, s32[2]{0:T(128)}, u32[]{:S(2)}) copy-start(s32[2]{0:T(128)} %param.13) | copy-start | bytes 28
  7.2 91.0 %copy-start.4 = (f32[1,512]{1,0:T(1,128)S(1)}, f32[1,512]{1,0:T(1,128)}, u32[]{:S(2)}) copy-start(f32[1,512]{1,0:T(1,128)} %param.16) | copy-start | bytes 6148
  7.2 129.1 %copy-start.3 = (f32[1,1024]{1,0:T(1,128)S(1)}, f32[1,1024]{1,0:T(1,128)}, u32[]{:S(2)}) copy-start(f32[1,1024]{1,0:T(1,128)} %param.17) | copy-start | bytes 12292
  7.2 211.8 %all-reduce.7.cloned.1.call-start = ((), (), s32[]{:S(2)}) async-start(), calls=%async_computation.1 | async-start | bytes 393216 | tf_op jit(solution)/shard_map/psum | solution.py:60
  51.1 170.1 %copy-start = (bf16[2,512,1024]{2,1,0:T(8,128)(2,1)S(1)}, bf16[2,512,1024]{2,1,0:T(8,128)(2,1)}, u32[]{:S(2)}) copy-start(bf16[2,512,1024]{2,1,0:T(8,128)(2,1)} %param.10) | copy-start | bytes 6291460
  98.1 255.8 %all-reduce.5.cloned.1.call-start = ((), (), s32[]{:S(2)}) async-start(), calls=%async_computation | async-start | bytes 393216 | tf_op jit(solution)/shard_map/psum | solution.py:60
Sparse Core Ops, SparseCore 0:
  98.2 120.6 all-reduce.6
  229.7 124.1 all-reduce.4
where the time goes:
time: 364 us; the launch traced here: 363 us
  waiting for transfers between devices  170 us (47%)
  blocking collectives  156 us (43%)
  other arithmetic  17 us (5%)
  between operations  14.1 us (4%)
  matrix products  5.92 us (2%)
    psum x2, waiting for transfers between devices, body(): row_total, col_total = lax.psum((row_blocks, col_blocks), 'tiles')  170 us
    all_gather x1, blocking collectives, body(): lax.all_gather(slot_dual, 'tiles', axis=0, tiled=True)  43.8 us
    all_gather x1, blocking collectives, body(): lax.all_gather(spend_limit, 'tiles', axis=0, tiled=True)  38.1 us
    all_gather x1, blocking collectives, body(): lax.all_gather(adv_dual, 'tiles', axis=0, tiled=True)  37.2 us
    all_gather x1, blocking collectives, body(): lax.all_gather(capacity, 'tiles', axis=0, tiled=True)  37 us
  transfers between devices with their start and end apart: 2, of which 2 were waited for; matrix products, arithmetic and copies ran while one was open for 0% of the time, Pallas kernels for 0%

commit v1 on v0

v1 whole, which is shorter than its diff:
```python
import functools

import jax
import jax.numpy as jnp
from jax import lax
from jax.experimental import pallas as pl
from jax.experimental.pallas import tpu as pltpu
from jax.sharding import PartitionSpec as P

ITERS = 2
LANES = 128
SUB = 8
STEP = 32
MESH = pl.DeviceIdType.MESH


def split_chips(chips):
    inner = 1
    for size in range(1, chips + 1):
        if size * size <= chips and chips % size == 0:
            inner = size
    return chips // inner, inner


class Gather:
    def __init__(self, buf, outer_sems, inner_sems, core_sems, place, sizes):
        self.buf = buf
        self.outer_sems, self.inner_sems, self.core_sems = outer_sems, inner_sems, core_sems
        self.o, self.i, self.c = place
        self.outer, self.inner = sizes
        self.sent = []

    def device(self, o, i, c):
        return ((o * self.inner + i) * 2 + c,)

    def back(self, at, k, size):
        return lax.rem(at - k + size, size)

    def copy(self, ref, sems, k, device, start):
        made = pltpu.make_async_remote_copy(
            src_ref=ref,
            dst_ref=ref,
            send_sem=sems.at[0, k],
            recv_sem=sems.at[1, k],
            device_id=device,
            device_id_type=MESH,
        )
        if start:
            made.start()
            self.sent.append(made)
        return made

    def start(self):
        for k in range(1, self.outer):
            to = self.device(lax.rem(self.o + k, self.outer), self.i, self.c)
            self.copy(self.buf.at[self.c, self.i, self.o], self.outer_sems, k, to, True)

    def to_partner(self, k):
        column = self.buf.at[self.c, self.back(self.i, k, self.inner)]
        self.copy(column, self.core_sems, k, self.device(self.o, self.i, 1 - self.c), True)

    def spread(self):
        for k in range(1, self.outer):
            block = self.buf.at[self.c, self.i, self.back(self.o, k, self.outer)]
            self.copy(block, self.outer_sems, k, self.device(self.o, self.i, 1 - self.c), False).wait_recv()
        for k in range(1, self.inner):
            to = self.device(self.o, lax.rem(self.i + k, self.inner), self.c)
            self.copy(self.buf.at[self.c, self.i], self.inner_sems, k, to, True)
        self.to_partner(0)

    def pass_on(self):
        for k in range(1, self.inner):
            column = self.buf.at[self.c, self.back(self.i, k, self.inner)]
            self.copy(column, self.inner_sems, k, self.device(self.o, self.i, 1 - self.c), False).wait_recv()
            self.to_partner(k)

    def finish(self):
        for k in range(self.inner):
            column = self.buf.at[1 - self.c, self.back(self.i, k, self.inner)]
            self.copy(column, self.core_sems, k, self.device(self.o, self.i, 1 - self.c), False).wait_recv()

    def drain(self):
        for made in self.sent:
            made.wait_send()


def kernel(
    outer, inner, cap, rows, cols,
    adv_id, slot_id, mask, adv_dual, slot_dual, limit, capacity, start_hbm, cost_hbm,
    primal_hbm, adv_out, slot_out,
    tile, price, weight, row_part, col_sum, row_sum, half_adv, half_slot, totals,
    dual_buf, rest_buf, sums_one, sums_two,
    outer_sems, inner_sems, core_sems, in_sems, out_sems,
):
    me = lax.axis_index("tiles")
    c = lax.rem(me, 2)
    i = lax.rem(me // 2, inner)
    o = me // (2 * inner)
    row_lines, col_lines = rows // LANES, cols // LANES
    groups = STEP // SUB
    mask_rows = mask.shape[1]

    loads = []
    for t in range(cap):
        pair = (
            pltpu.make_async_copy(start_hbm.at[t], tile.at[t], in_sems.at[0, t]),
            pltpu.make_async_copy(cost_hbm.at[t], price.at[t], in_sems.at[1, t]),
        )
        for made in pair:
            made.start()
        loads.append(pair)

    barrier = pltpu.get_barrier_semaphore()
    peers = [((lax.rem(o + k, outer) * inner + i) * 2 + c) for k in range(1, outer)]
    peers += [((o * inner + lax.rem(i + k, inner)) * 2 + c) for k in range(1, inner)]
    peers += [(o * inner + i) * 2 + 1 - c]
    for peer in peers:
        pl.semaphore_signal(barrier, inc=1, device_id=(peer,), device_id_type=MESH)

    gathers = [
        Gather(buf, outer_sems.at[g], inner_sems.at[g], core_sems.at[g], (o, i, c), (outer, inner))
        for g, buf in enumerate((dual_buf, rest_buf, sums_one, sums_two))
    ]
    duals, rest, first, second = gathers

    for r in range(row_lines):
        at = slice(r * LANES, (r + 1) * LANES)
        dual_buf[c, i, o, r:r + 1, :] = adv_dual[0:1, at]
        dual_buf[c, i, o, row_lines + r:row_lines + r + 1, :] = limit[0:1, at]
    for r in range(col_lines):
        at = slice(r * LANES, (r + 1) * LANES)
        dual_buf[c, i, o, 2 * row_lines + r:2 * row_lines + r + 1, :] = slot_dual[0:1, at]
        rest_buf[c, i, o, r:r + 1, :] = capacity[0:1, at]
    for t in range(cap):
        rest_buf[c, i, o, col_lines + t:col_lines + t + 1, :] = jnp.full(
            (1, LANES), adv_id[t].astype(jnp.float32))
        rest_buf[c, i, o, col_lines + cap + t:col_lines + cap + t + 1, :] = jnp.full(
            (1, LANES), slot_id[t].astype(jnp.float32))

    pl.semaphore_wait(barrier, len(peers))
    duals.start()
    rest.start()

    for t in range(cap):
        alive = jnp.where(adv_id[t] >= 0, 1.0, 0.0).astype(jnp.float32)
        blocks = mask[t].astype(jnp.float32) * alive
        for j in range(mask.shape[2]):
            weight[t, j] = jnp.broadcast_to(blocks[:, j:j + 1], (mask_rows, LANES))

    def exists(t, at, j):
        return jnp.broadcast_to(weight[t, j, pl.ds(at, 1), :], (SUB, LANES))

    def sum_tile(t, value):
        def step(s, col):
            col = list(col)
            for g in range(groups):
                row = None
                for j in range(col_lines):
                    piece = value(s, g, j)
                    row = piece if row is None else row + piece
                    col[j] = col[j] + piece
                row_part[t, pl.ds(s * STEP + g * SUB, SUB), :] = row
            return tuple(col)

        zero = jnp.zeros((SUB, LANES), jnp.float32)
        return lax.fori_loop(0, rows // STEP, step, (zero,) * col_lines)

    def keep_sums(slot, t, col):
        for r in range(row_lines):
            turned = jnp.transpose(row_part[t, r * LANES:(r + 1) * LANES, :])
            row_sum[slot, t * row_lines + r:t * row_lines + r + 1, :] = jnp.sum(turned, axis=0, keepdims=True)
        for j in range(col_lines):
            col_sum[slot, t, j:j + 1, :] = jnp.sum(col[j], axis=0, keepdims=True)

    def prepare(t):
        for made in loads[t]:
            made.wait()

        def step(s, col):
            col = list(col)
            for h in range(STEP // 16):
                row = [None, None]
                for j in range(col_lines):
                    at = (t, pl.ds(s * STEP + h * 16, 16), slice(j * LANES, (j + 1) * LANES))
                    x = tile[at]
                    tile[at] = x - 0.5 * price[at].astype(jnp.float32)
                    for half in range(2):
                        piece = x[half * SUB:(half + 1) * SUB] * exists(t, s * groups + h * 2 + half, j)
                        row[half] = piece if row[half] is None else row[half] + piece
                        col[j] = col[j] + piece
                for half in range(2):
                    row_part[t, pl.ds(s * STEP + h * 16 + half * SUB, SUB), :] = row[half]
            return tuple(col)

        zero = jnp.zeros((SUB, LANES), jnp.float32)
        keep_sums(0, t, lax.fori_loop(0, rows // STEP, step, (zero,) * col_lines))

    def less_price(t):
        def step(s, carry):
            for h in range(STEP // 16):
                for j in range(col_lines):
                    at = (t, pl.ds(s * STEP + h * 16, 16), slice(j * LANES, (j + 1) * LANES))
                    tile[at] = tile[at] - 0.5 * price[at].astype(jnp.float32)
            return carry

        lax.fori_loop(0, rows // STEP, step, 0)

    def set_duals(t, adv, slot):
        for r in range(row_lines):
            spread = jnp.broadcast_to(0.5 * adv[r:r + 1, :], (LANES, LANES))
            half_adv[t, r * LANES:(r + 1) * LANES, :] = jnp.transpose(spread)
        half_slot[t] = 0.5 * slot

    def update(t, slot):
        slots = [jnp.broadcast_to(half_slot[t, j:j + 1, :], (SUB, LANES)) for j in range(col_lines)]

        def value(s, g, j):
            at = (t, pl.ds(s * STEP + g * SUB, SUB), slice(j * LANES, (j + 1) * LANES))
            moved = tile[at] - half_adv[t, pl.ds(s * STEP + g * SUB, SUB), :] - slots[j]
            new = jnp.clip(moved, 0.0, 1.0) * exists(t, s * groups + g, j)
            tile[at] = new
            return new

        keep_sums(slot, t, sum_tile(t, value))

    def post(buf, slot):
        buf[c, i, o, 0:cap * row_lines, :] = 2.0 * row_sum[slot] - row_sum[slot - 1]
        for t in range(cap):
            at = cap * row_lines + t * col_lines
            buf[c, i, o, at:at + col_lines, :] = 2.0 * col_sum[slot, t] - col_sum[slot - 1, t]

    def add_up(buf, targets):
        wanted = [
            (jnp.full((1, LANES), a.astype(jnp.float32)), jnp.full((1, LANES), b.astype(jnp.float32)))
            for a, b in targets
        ]

        def step(m, sums):
            sums = list(sums)
            cc, ii = m // inner, lax.rem(m, inner)
            for oo in range(outer):
                for t in range(cap):
                    a_of = rest_buf[cc, ii, oo, col_lines + t:col_lines + t + 1, :]
                    s_of = rest_buf[cc, ii, oo, col_lines + cap + t:col_lines + cap + t + 1, :]
                    by_row = buf[cc, ii, oo, t * row_lines:(t + 1) * row_lines, :]
                    at = cap * row_lines + t * col_lines
                    by_col = buf[cc, ii, oo, at:at + col_lines, :]
                    for k, (a, b) in enumerate(wanted):
                        hit_a = jnp.where(a_of == a, 1.0, 0.0)
                        hit_b = jnp.where(s_of == b, 1.0, 0.0)
                        sums[2 * k] = sums[2 * k] + by_row * hit_a
                        sums[2 * k + 1] = sums[2 * k + 1] + by_col * hit_b
            return tuple(sums)

        begin = []
        for _ in targets:
            begin += [jnp.zeros((row_lines, LANES), jnp.float32), jnp.zeros((col_lines, LANES), jnp.float32)]
        return lax.fori_loop(0, 2 * inner, step, tuple(begin))

    def place(block):
        return lax.rem(block, 2), lax.rem(block // 2, inner), block // (2 * inner)

    def old_adv(block):
        at = place(block)
        return dual_buf[at + (slice(0, row_lines),)], dual_buf[at + (slice(row_lines, 2 * row_lines),)]

    def old_slot(block):
        at = place(block)
        return dual_buf[at + (slice(2 * row_lines, 2 * row_lines + col_lines),)], rest_buf[at + (slice(0, col_lines),)]

    ids = [(jnp.maximum(adv_id[t], 0), jnp.maximum(slot_id[t], 0)) for t in range(cap)]

    prepare(0)
    duals.spread()
    rest.spread()
    for t in range(1, cap):
        prepare(t)
    duals.pass_on()
    duals.finish()

    for t in range(cap):
        set_duals(t, old_adv(ids[t][0])[0], old_slot(ids[t][1])[0])
    for t in range(cap):
        update(t, 1)
    post(sums_one, 1)
    first.start()
    rest.pass_on()
    less_price(0)
    first.spread()
    for t in range(1, cap):
        less_price(t)
    first.pass_on()
    rest.finish()
    first.finish()

    targets = ids + [(me, me)]
    sums = add_up(sums_one, targets)
    for k, (a, b) in enumerate(targets):
        adv, lim = old_adv(a)
        slot, room = old_slot(b)
        adv = jnp.maximum(adv + (sums[2 * k] - lim) / cols, 0.0)
        slot = jnp.maximum(slot + (sums[2 * k + 1] - room) / rows, 0.0)
        if k < cap:
            set_duals(k, adv, slot)
        else:
            totals[0:row_lines, :] = adv
            totals[row_lines:row_lines + col_lines, :] = slot

    stores = []
    for t in range(cap):
        update(t, 2)
        made = pltpu.make_async_copy(tile.at[t], primal_hbm.at[t], out_sems.at[t])
        made.start()
        stores.append(made)
    post(sums_two, 2)
    second.start()
    second.spread()
    second.pass_on()
    second.finish()

    row_use, col_use = add_up(sums_two, [(me, me)])
    adv = jnp.maximum(totals[0:row_lines, :] + (row_use - old_adv(me)[1]) / cols, 0.0)
    slot = jnp.maximum(
        totals[row_lines:row_lines + col_lines, :] + (col_use - old_slot(me)[1]) / rows, 0.0)
    for r in range(row_lines):
        adv_out[0:1, r * LANES:(r + 1) * LANES] = adv[r:r + 1, :]
    for r in range(col_lines):
        slot_out[0:1, r * LANES:(r + 1) * LANES] = slot[r:r + 1, :]

    for gather in gathers:
        gather.drain()
    for made in stores:
        made.wait()


def body(primal_start, cost, mask, tile_adv, tile_slot, adv_dual, slot_dual, spend_limit, capacity):
    devices = lax.axis_size("tiles")
    outer, inner = split_chips(devices // 2)
    cap, rows, cols = primal_start.shape
    row_lines, col_lines = rows // LANES, cols // LANES
    f32 = jnp.float32
    spread = (2, inner, outer)
    dual_lines = 2 * row_lines + col_lines
    rest_lines = col_lines + -(-2 * cap // SUB) * SUB
    sum_lines = cap * (row_lines + col_lines)
    vmem = pl.BlockSpec(memory_space=pltpu.VMEM)
    smem = pl.BlockSpec(memory_space=pltpu.SMEM)
    hbm = pl.BlockSpec(memory_space=pl.ANY)
    return pl.pallas_call(
        functools.partial(kernel, outer, inner, cap, rows, cols),
        out_shape=(
            jax.ShapeDtypeStruct(primal_start.shape, f32),
            jax.ShapeDtypeStruct(adv_dual.shape, f32),
            jax.ShapeDtypeStruct(slot_dual.shape, f32),
        ),
        in_specs=[smem, smem, vmem, vmem, vmem, vmem, vmem, hbm, hbm],
        out_specs=(hbm, vmem, vmem),
        scratch_shapes=[
            pltpu.VMEM((cap, rows, cols), f32),
            pltpu.VMEM((cap, rows, cols), cost.dtype),
            pltpu.VMEM((cap, mask.shape[2], mask.shape[1], LANES), f32),
            pltpu.VMEM((cap, rows, LANES), f32),
            pltpu.VMEM((ITERS + 1, cap, col_lines, LANES), f32),
            pltpu.VMEM((ITERS + 1, cap * row_lines, LANES), f32),
            pltpu.VMEM((cap, rows, LANES), f32),
            pltpu.VMEM((cap, col_lines, LANES), f32),
            pltpu.VMEM((row_lines + col_lines, LANES), f32),
            pltpu.VMEM(spread + (dual_lines, LANES), f32),
            pltpu.VMEM(spread + (rest_lines, LANES), f32),
            pltpu.VMEM(spread + (sum_lines, LANES), f32),
            pltpu.VMEM(spread + (sum_lines, LANES), f32),
            pltpu.SemaphoreType.DMA((4, 2, outer)),
            pltpu.SemaphoreType.DMA((4, 2, inner)),
            pltpu.SemaphoreType.DMA((4, 2, inner)),
            pltpu.SemaphoreType.DMA((2, cap)),
            pltpu.SemaphoreType.DMA((cap,)),
        ],
        compiler_params=pltpu.CompilerParams(
            collective_id=0, has_side_effects=True, vmem_limit_bytes=40 * 1024 * 1024
        ),
    )(tile_adv, tile_slot, mask, adv_dual, slot_dual, spend_limit, capacity, primal_start, cost)


def solution(mesh):
    return jax.shard_map(
        body,
        mesh=mesh,
        in_specs=(
            P("tiles", None, None),
            P("tiles", None, None),
            P("tiles", None, None),
            P("tiles"),
            P("tiles"),
            P("tiles", None),
            P("tiles", None),
            P("tiles", None),
            P("tiles", None),
        ),
        out_specs=(P("tiles", None, None), P("tiles", None), P("tiles", None)),
        check_vma=False,
    )
```

time: 364 us -> 49.6 us (0.14)
  waiting for transfers between devices: 170 us -> 0 us
  blocking collectives: 156 us -> 0 us
  Pallas kernels: 0 us -> 36.7 us
  other arithmetic: 17 us -> 0 us
  between operations: 14.1 us -> 0.66 us
  local copies, waits for them, and re-layouts: 0.15 us -> 11.8 us
  matrix products: 5.92 us -> 0 us
    psum x2 -> x0, waiting for transfers between devices: 170 us -> none  [body(): row_total, col_total = lax.psum((row_blocks, col_blocks), 'tiles')]
    all_gather x4 -> x0, blocking collectives: 156 us -> none  [the longest x1 43.8 us: body(): lax.all_gather(slot_dual, 'tiles', axis=0, tiled=True)]
    pallas_call x0 -> x1, Pallas kernels: none -> 36.7 us  [body(): pl.pallas_call(functools.partial(kernel, outer, inner, cap, rows, cols),...]
    unnamed x12 -> x20, local copies, waits for them, and re-layouts: 0.06 us -> 11.8 us
    reduce_sum x2 -> x0, other arithmetic: 11.1 us -> none  [the longest x1 6.38 us: body(): jnp.sum(extended, axis=1)]
    dot_general x8 -> x0, matrix products: 5.92 us -> none  [the longest x2 1.97 us: body(): jnp.dot(slot_onehot.T, jnp.sum(extended, axis=1), precision=highest)]
    max x4 -> x0, other arithmetic: 4.5 us -> none  [the longest x2 2.33 us: body(): jnp.maximum(slot_all + (col_total - capacity_all) / rows_tile, 0.0)]
  transfers between devices with their start and end apart: 2 -> 0, of which waited for: 2 -> 0; matrix products, arithmetic and copies ran while one was open for 0% -> 0% of each run, Pallas kernels for 0% -> 0%
where the time goes in v1:
time: 49.6 us; the launch traced here: 49.1 us
  Pallas kernels  36.7 us (74%)
  local copies, waits for them, and re-layouts  11.8 us (24%)
  between operations  0.66 us (1%)
    pallas_call x1, Pallas kernels, body(): pl.pallas_call(functools.partial(kernel, outer, inner, cap, rows, cols),...  36.7 us
    unnamed x20, local copies, waits for them, and re-layouts  11.8 us

profile of v1, /device:TPU:0, one launch (start us, length us, event | category | flops | bytes accessed | tf_op | source)
XLA Modules:
  0.0 49.1 jit_solution(8890626657433280838)
XLA Ops:
  0.6 0.8 %copy.12.mask = s32[2,64,8]{2,1,0:T(8,128)S(1)} copy(s32[2,64,8]{1,2,0:T(8,128)} %param.11) | data formatting | bytes 8192 | tf_op args[2]
  1.4 0.0 copy-start
  1.4 2.2 %copy-done = f32[2,512,1024]{2,1,0:T(8,128)S(1)} copy-done((f32[2,512,1024]{2,1,0:T(8,128)S(1)}, f32[2,512,1024]{2,1,0:T(8,128)}, u32[]{:S(2)}) %copy-start) | copy-done | bytes 4194328
  3.6 0.0 copy-start.1
  3.6 1.6 %copy-done.1 = bf16[2,512,1024]{2,1,0:T(8,128)(2,1)S(1)} copy-done((bf16[2,512,1024]{2,1,0:T(8,128)(2,1)S(1)}, bf16[2,512,1024]{2,1,0:T(8,128)(2,1)}, u32[]{:S(2)}) %copy-start.1) | copy-done | bytes 2097176
  5.2 0.0 copy-start.2
  5.2 0.7 %copy-done.2 = f32[1,1024]{1,0:T(1,128)S(1)} copy-done((f32[1,1024]{1,0:T(1,128)S(1)}, f32[1,1024]{1,0:T(1,128)}, u32[]{:S(2)}) %copy-start.2) | copy-done | bytes 4120
  5.9 0.0 copy-start.3
  5.9 0.7 %copy-done.3 = f32[1,1024]{1,0:T(1,128)S(1)} copy-done((f32[1,1024]{1,0:T(1,128)S(1)}, f32[1,1024]{1,0:T(1,128)}, u32[]{:S(2)}) %copy-start.3) | copy-done | bytes 4120
  6.6 0.0 copy-start.4
  6.6 0.7 %copy-done.4 = f32[1,512]{1,0:T(1,128)S(1)} copy-done((f32[1,512]{1,0:T(1,128)S(1)}, f32[1,512]{1,0:T(1,128)}, u32[]{:S(2)}) %copy-start.4) | copy-done | bytes 2072
  7.3 0.0 copy-start.5
  7.3 0.7 %copy-done.5 = f32[1,512]{1,0:T(1,128)S(1)} copy-done((f32[1,512]{1,0:T(1,128)S(1)}, f32[1,512]{1,0:T(1,128)}, u32[]{:S(2)}) %copy-start.5) | copy-done | bytes 2072
  7.9 0.0 copy-start.6
  7.9 0.7 %copy-done.6 = s32[2]{0:T(128)S(1)} copy-done((s32[2]{0:T(128)S(1)}, s32[2]{0:T(128)}, u32[]{:S(2)}) %copy-start.6) | copy-done | bytes 32
  8.6 0.0 copy-start.7
  8.6 0.7 %copy-done.7 = s32[2]{0:T(128)S(1)} copy-done((s32[2]{0:T(128)S(1)}, s32[2]{0:T(128)}, u32[]{:S(2)}) %copy-start.7) | copy-done | bytes 32
  9.3 36.7 %shard_map.112 = (f32[2,512,1024]{2,1,0:T(8,128)S(1)}, f32[1,512]{1,0:T(1,128)S(1)}, f32[1,1024]{1,0:T(1,128)S(1)}) custom-call(s32[2]{0:T(128)S(1)} %copy-done.6, s32[2]{0:T(128)S(1)} %copy-done.7, s32[2,64,8]{2,1,0:T(8,128)S(1)} %copy.12.mask, f32[1,512]{1,0:T(1,128)S(1)} %copy-done.4, f32[1,1024]{1,0:T(1,128)S(1)} %copy-done.2, f32[1,512]{1,0:T(1,128)S(1)} %copy-done.5, ...), custom_call_target="tpu_custom_call" | custom-call | tf_op jit(solution)/shard_map/pallas_call | solution.py:349
  46.0 2.0 %copy.16 = f32[2,512,1024]{2,1,0:T(8,128)} copy(f32[2,512,1024]{2,1,0:T(8,128)S(1)} %get-tuple-element.6) | data formatting | bytes 8388608
  48.0 0.6 %copy.17 = f32[1,512]{1,0:T(1,128)} copy(f32[1,512]{1,0:T(1,128)S(1)} %get-tuple-element.7) | data formatting | bytes 4096
  48.5 0.6 %copy.18 = f32[1,1024]{1,0:T(1,128)} copy(f32[1,1024]{1,0:T(1,128)S(1)} %get-tuple-element.8) | data formatting | bytes 8192
Async XLA Ops:
  1.4 2.2 %copy-start = (f32[2,512,1024]{2,1,0:T(8,128)S(1)}, f32[2,512,1024]{2,1,0:T(8,128)}, u32[]{:S(2)}) copy-start(f32[2,512,1024]{2,1,0:T(8,128)} %start_hbm.1) | copy-start | bytes 12582916
  3.6 1.6 %copy-start.1 = (bf16[2,512,1024]{2,1,0:T(8,128)(2,1)S(1)}, bf16[2,512,1024]{2,1,0:T(8,128)(2,1)}, u32[]{:S(2)}) copy-start(bf16[2,512,1024]{2,1,0:T(8,128)(2,1)} %cost_hbm.1) | copy-start | bytes 6291460
  5.2 0.7 %copy-start.2 = (f32[1,1024]{1,0:T(1,128)S(1)}, f32[1,1024]{1,0:T(1,128)}, u32[]{:S(2)}) copy-start(f32[1,1024]{1,0:T(1,128)} %slot_dual.1) | copy-start | bytes 12292
  5.9 0.7 %copy-start.3 = (f32[1,1024]{1,0:T(1,128)S(1)}, f32[1,1024]{1,0:T(1,128)}, u32[]{:S(2)}) copy-start(f32[1,1024]{1,0:T(1,128)} %capacity.1) | copy-start | bytes 12292
  6.6 0.7 %copy-start.4 = (f32[1,512]{1,0:T(1,128)S(1)}, f32[1,512]{1,0:T(1,128)}, u32[]{:S(2)}) copy-start(f32[1,512]{1,0:T(1,128)} %adv_dual.1) | copy-start | bytes 6148
  7.3 0.7 %copy-start.5 = (f32[1,512]{1,0:T(1,128)S(1)}, f32[1,512]{1,0:T(1,128)}, u32[]{:S(2)}) copy-start(f32[1,512]{1,0:T(1,128)} %limit.1) | copy-start | bytes 6148
  7.9 0.7 %copy-start.6 = (s32[2]{0:T(128)S(1)}, s32[2]{0:T(128)}, u32[]{:S(2)}) copy-start(s32[2]{0:T(128)} %adv_id.1) | copy-start | bytes 28
  8.6 0.7 %copy-start.7 = (s32[2]{0:T(128)S(1)}, s32[2]{0:T(128)}, u32[]{:S(2)}) copy-start(s32[2]{0:T(128)} %slot_id.1) | copy-start | bytes 28

commit v2 on v1

v2 whole, which is shorter than its diff:
```python
import functools

import jax
import jax.numpy as jnp
from jax import lax
from jax.experimental import pallas as pl
from jax.experimental.pallas import tpu as pltpu
from jax.sharding import PartitionSpec as P

ITERS = 2
LANES = 128
SUB = 8
STEP = 32
MESH = pl.DeviceIdType.MESH


def split_chips(chips):
    inner = 1
    for size in range(1, chips + 1):
        if size * size <= chips and chips % size == 0:
            inner = size
    return chips // inner, inner


class Copies:
    def __init__(self, sems):
        self.sems = sems
        self.made = {}

    def start(self, k, src, dst, device):
        made = pltpu.make_async_remote_copy(
            src_ref=src,
            dst_ref=dst,
            send_sem=self.sems.at[0, k],
            recv_sem=self.sems.at[1, k],
            device_id=(device,),
            device_id_type=MESH,
        )
        made.start()
        self.made[k] = made

    def arrive(self):
        for made in self.made.values():
            made.wait_recv()

    def drain(self):
        for made in self.made.values():
            made.wait_send()


def kernel(
    outer, inner, cap, rows, cols,
    adv_id, slot_id, mask_hbm, adv_hbm, slot_hbm, limit_hbm, room_hbm, start_hbm, cost_hbm,
    primal_hbm, adv_out, slot_out,
    tile, price, blocks, adv_dual, slot_dual, limit, capacity, square, weight, row_part, col_sum, row_sum,
    half_adv, half_slot, totals, dual_buf, rest_buf, sums_one, sums_two, ids_buf,
    send_start, send_one, send_two, got_start, got_one, got_two,
    column_sems, plane_sems, in_sems, small_sems, out_sems,
):
    plane = 2 * inner
    me = lax.axis_index("tiles")
    p = lax.rem(me, plane)
    o = me // plane
    row_lines, col_lines = rows // LANES, cols // LANES
    groups = STEP // SUB
    mask_rows, mask_cols = mask_hbm.shape[2], mask_hbm.shape[1]

    small = [
        pltpu.make_async_copy(src, dst, small_sems.at[n])
        for n, (src, dst) in enumerate((
            (adv_hbm, adv_dual), (slot_hbm, slot_dual), (limit_hbm, limit), (room_hbm, capacity), (mask_hbm, blocks)))
    ]
    for made in small:
        made.start()
    loads = []
    for t in range(cap):
        pair = (
            pltpu.make_async_copy(start_hbm.at[t], tile.at[t], in_sems.at[0, t]),
            pltpu.make_async_copy(cost_hbm.at[t], price.at[t], in_sems.at[1, t]),
        )
        for made in pair:
            made.start()
        loads.append(pair)

    def in_column(k):
        return lax.rem(o + k, outer) * plane + p

    def in_plane(k):
        return o * plane + lax.rem(p + k, plane)

    barrier = pltpu.get_barrier_semaphore()
    peers = [in_column(k) for k in range(1, outer)] + [in_plane(k) for k in range(1, plane)]
    for peer in peers:
        pl.semaphore_signal(barrier, inc=1, device_id=(peer,), device_id_type=MESH)

    exchanges = [Copies(column_sems.at[g]) for g in range(4)] + [Copies(plane_sems.at[g]) for g in range(4)]
    duals, rest, first, second, named, part_start, part_one, part_two = exchanges

    def slot_at(e):
        return slice(e * col_lines, (e + 1) * col_lines)

    def adv_at(n, e):
        return slice(n * col_lines + e * row_lines, n * col_lines + (e + 1) * row_lines)

    id_line = col_lines + row_lines
    for t in range(cap):
        for n, ids in ((t, adv_id), (cap + t, slot_id)):
            value = jnp.full((1, LANES), ids[t].astype(jnp.float32))
            ids_buf[p, n:n + 1, :] = value
            rest_buf[o, id_line + n:id_line + n + 1, :] = value
    for made in small[:4]:
        made.wait()
    for r in range(row_lines):
        at = slice(r * LANES, (r + 1) * LANES)
        dual_buf[o, col_lines + r:col_lines + r + 1, :] = adv_dual[0:1, at]
        rest_buf[o, col_lines + r:col_lines + r + 1, :] = limit[0:1, at]
    for r in range(col_lines):
        at = slice(r * LANES, (r + 1) * LANES)
        dual_buf[o, r:r + 1, :] = slot_dual[0:1, at]
        rest_buf[o, r:r + 1, :] = capacity[0:1, at]

    def send_column(copies, buf):
        for k in range(outer - 1, 0, -1):
            copies.start(k, buf.at[o], buf.at[o], in_column(k))

    pl.semaphore_wait(barrier, len(peers))
    send_column(duals, dual_buf)
    for k in range(1, plane):
        named.start(k, ids_buf.at[p], ids_buf.at[p], in_plane(k))
    send_column(rest, rest_buf)

    small[4].wait()
    square[...] = jnp.zeros_like(square)
    for t in range(cap):
        alive = jnp.where(adv_id[t] >= 0, 1.0, 0.0).astype(jnp.float32)
        square[0:mask_cols, 0:mask_rows] = blocks[t].astype(jnp.float32) * alive
        turned = jnp.transpose(square[...])
        for j in range(mask_cols):
            weight[t, j] = jnp.broadcast_to(turned[0:mask_rows, j:j + 1], (mask_rows, LANES))

    def exists(t, at, j):
        return jnp.broadcast_to(weight[t, j, pl.ds(at, 1), :], (SUB, LANES))

    def sum_tile(t, value):
        def step(s, col):
            col = list(col)
            for g in range(groups):
                row = None
                for j in range(col_lines):
                    piece = value(s, g, j)
                    row = piece if row is None else row + piece
                    col[j] = col[j] + piece
                row_part[t, pl.ds(s * STEP + g * SUB, SUB), :] = row
            return tuple(col)

        zero = jnp.zeros((SUB, LANES), jnp.float32)
        return lax.fori_loop(0, rows // STEP, step, (zero,) * col_lines)

    def keep_sums(slot, t, col):
        for r in range(row_lines):
            turned = jnp.transpose(row_part[t, r * LANES:(r + 1) * LANES, :])
            row_sum[slot, t * row_lines + r:t * row_lines + r + 1, :] = jnp.sum(turned, axis=0, keepdims=True)
        for j in range(col_lines):
            col_sum[slot, t, j:j + 1, :] = jnp.sum(col[j], axis=0, keepdims=True)

    def prepare(t):
        for made in loads[t]:
            made.wait()

        def step(s, col):
            col = list(col)
            for h in range(STEP // 16):
                row = [None, None]
                for j in range(col_lines):
                    at = (t, pl.ds(s * STEP + h * 16, 16), slice(j * LANES, (j + 1) * LANES))
                    x = tile[at]
                    tile[at] = x - 0.5 * price[at].astype(jnp.float32)
                    for half in range(2):
                        piece = x[half * SUB:(half + 1) * SUB] * exists(t, s * groups + h * 2 + half, j)
                        row[half] = piece if row[half] is None else row[half] + piece
                        col[j] = col[j] + piece
                for half in range(2):
                    row_part[t, pl.ds(s * STEP + h * 16 + half * SUB, SUB), :] = row[half]
            return tuple(col)

        zero = jnp.zeros((SUB, LANES), jnp.float32)
        keep_sums(0, t, lax.fori_loop(0, rows // STEP, step, (zero,) * col_lines))

    def less_price(t):
        def step(s, carry):
            for h in range(STEP // 16):
                for j in range(col_lines):
                    at = (t, pl.ds(s * STEP + h * 16, 16), slice(j * LANES, (j + 1) * LANES))
                    tile[at] = tile[at] - 0.5 * price[at].astype(jnp.float32)
            return carry

        lax.fori_loop(0, rows // STEP, step, 0)

    def set_duals(t, adv, slot):
        for r in range(row_lines):
            spread = jnp.broadcast_to(0.5 * adv[r:r + 1, :], (LANES, LANES))
            half_adv[t, r * LANES:(r + 1) * LANES, :] = jnp.transpose(spread)
        half_slot[t] = 0.5 * slot

    def update(t, slot):
        slots = [jnp.broadcast_to(half_slot[t, j:j + 1, :], (SUB, LANES)) for j in range(col_lines)]

        def value(s, g, j):
            at = (t, pl.ds(s * STEP + g * SUB, SUB), slice(j * LANES, (j + 1) * LANES))
            moved = tile[at] - half_adv[t, pl.ds(s * STEP + g * SUB, SUB), :] - slots[j]
            new = jnp.clip(moved, 0.0, 1.0) * exists(t, s * groups + g, j)
            tile[at] = new
            return new

        keep_sums(slot, t, sum_tile(t, value))

    def post(buf, slot):
        for t in range(cap):
            at = slice(t * row_lines, (t + 1) * row_lines)
            buf[o, slot_at(t), :] = 2.0 * col_sum[slot, t] - col_sum[slot - 1, t]
            buf[o, adv_at(cap, t), :] = 2.0 * row_sum[slot, at, :] - row_sum[slot - 1, at, :]

    def splat(value):
        return jnp.full((1, LANES), value.astype(jnp.float32))

    def tile_items(buf):
        return [
            (
                rest_buf[b, id_line + t:id_line + t + 1, :], rest_buf[b, id_line + cap + t:id_line + cap + t + 1, :],
                buf[b, adv_at(cap, t), :], buf[b, slot_at(t), :],
            )
            for b in range(outer) for t in range(cap)
        ]

    def block_items(buf, sign):
        return [
            (splat(b * plane + p), splat(b * plane + p), sign * buf[b, adv_at(1, 0), :], sign * buf[b, slot_at(0), :])
            for b in range(outer)
        ]

    def targets_of(q, own):
        found = []
        if own != "alone":
            found = [(ids_buf[q, t:t + 1, :], ids_buf[q, cap + t:cap + t + 1, :]) for t in range(cap)]
        if own:
            found.append((splat(o * plane + q),) * 2)
        return found

    def part(items, targets, into, add):
        n = len(targets)
        for e, (a, b) in enumerate(targets):
            adv = into[adv_at(n, e), :] if add else jnp.zeros((row_lines, LANES), jnp.float32)
            slot = into[slot_at(e), :] if add else jnp.zeros((col_lines, LANES), jnp.float32)
            for a_of, b_of, by_row, by_col in items:
                adv = adv + jnp.where(a_of == a, 1.0, 0.0) * by_row
                slot = slot + jnp.where(b_of == b, 1.0, 0.0) * by_col
            into[adv_at(n, e), :] = adv
            into[slot_at(e), :] = slot

    def parts(copies, items, own, send, got, add=False, go=True):
        order = list(range(plane - 1, -1, -1))
        for k in order:
            into = send.at[k] if k else got.at[0]
            part(items, targets_of(lax.rem(p + k, plane), own), into, add)
            if go and k:
                copies.start(k, send.at[k], got.at[k], in_plane(k))

    def total(got):
        value = got[0]
        for k in range(1, plane):
            value = value + got[k]
        return value

    prepare(0)
    named.arrive()
    duals.arrive()
    parts(part_start, block_items(dual_buf, 1.0), False, send_start, got_start)
    for t in range(1, cap):
        prepare(t)
    rest.arrive()
    part_start.arrive()

    old = total(got_start)
    for t in range(cap):
        set_duals(t, old[adv_at(cap, t)], old[slot_at(t)])
    for t in range(cap):
        update(t, 1)
    post(sums_one, 1)
    send_column(first, sums_one)
    parts(part_one, block_items(rest_buf, -1.0), True, send_one, got_one, go=False)
    less_price(0)
    first.arrive()
    parts(part_one, tile_items(sums_one), True, send_one, got_one, add=True)
    for t in range(1, cap):
        less_price(t)
    part_one.arrive()

    moved = total(got_one)
    for k in range(cap + 1):
        adv, slot = moved[adv_at(cap + 1, k)], moved[slot_at(k)]
        if k < cap:
            adv = jnp.maximum(old[adv_at(cap, k)] + adv / cols, 0.0)
            slot = jnp.maximum(old[slot_at(k)] + slot / rows, 0.0)
            set_duals(k, adv, slot)
        else:
            totals[adv_at(1, 0), :] = jnp.maximum(dual_buf[o, adv_at(1, 0), :] + adv / cols, 0.0)
            totals[slot_at(0), :] = jnp.maximum(dual_buf[o, slot_at(0), :] + slot / rows, 0.0)

    stores = []
    for t in range(cap):
        update(t, 2)
        made = pltpu.make_async_copy(tile.at[t], primal_hbm.at[t], out_sems.at[t])
        made.start()
        stores.append(made)
    post(sums_two, 2)
    send_column(second, sums_two)
    second.arrive()
    parts(part_two, tile_items(sums_two), "alone", send_two, got_two)
    part_two.arrive()

    use = total(got_two)
    adv = totals[adv_at(1, 0), :] + (use[adv_at(1, 0)] - rest_buf[o, adv_at(1, 0), :]) / cols
    slot = totals[slot_at(0), :] + (use[slot_at(0)] - rest_buf[o, slot_at(0), :]) / rows
    for r in range(row_lines):
        adv_out[0:1, r * LANES:(r + 1) * LANES] = jnp.maximum(adv[r:r + 1, :], 0.0)
    for r in range(col_lines):
        slot_out[0:1, r * LANES:(r + 1) * LANES] = jnp.maximum(slot[r:r + 1, :], 0.0)

    for copies in exchanges:
        copies.drain()
    for made in stores:
        made.wait()


def store(*refs):
    pieces = refs[-1].shape[0] - 2
    cap, rows = refs[0].shape[:2]
    size = cap * rows // pieces
    made = []
    for n in range(pieces):
        at = (n * size // rows, pl.ds(n * size % rows, size))
        made.append(pltpu.make_async_copy(refs[0].at[at], refs[3].at[at], refs[-1].at[n]))
    made.append(pltpu.make_async_copy(refs[1], refs[4], refs[-1].at[pieces]))
    made.append(pltpu.make_async_copy(refs[2], refs[5], refs[-1].at[pieces + 1]))
    for copy in made:
        copy.start()
    for copy in made:
        copy.wait()


def body(primal_start, cost, mask, tile_adv, tile_slot, adv_dual, slot_dual, spend_limit, capacity):
    devices = lax.axis_size("tiles")
    outer, inner = split_chips(devices // 2)
    plane = 2 * inner
    cap, rows, cols = primal_start.shape
    row_lines, col_lines = rows // LANES, cols // LANES
    entry = row_lines + col_lines
    f32 = jnp.float32
    vmem = pl.BlockSpec(memory_space=pltpu.VMEM)
    smem = pl.BlockSpec(memory_space=pltpu.SMEM)
    hbm = pl.BlockSpec(memory_space=pltpu.HBM)
    mask = jnp.swapaxes(mask, 1, 2)
    outs = (
        jax.ShapeDtypeStruct(primal_start.shape, f32),
        jax.ShapeDtypeStruct(adv_dual.shape, f32),
        jax.ShapeDtypeStruct(slot_dual.shape, f32),
    )
    results = pl.pallas_call(
        functools.partial(kernel, outer, inner, cap, rows, cols),
        out_shape=outs,
        in_specs=[smem, smem, hbm, hbm, hbm, hbm, hbm, hbm, hbm],
        out_specs=(hbm, vmem, vmem),
        scratch_shapes=[
            pltpu.VMEM((cap, rows, cols), f32),
            pltpu.VMEM((cap, rows, cols), cost.dtype),
            pltpu.VMEM(mask.shape, mask.dtype),
            pltpu.VMEM(adv_dual.shape, f32),
            pltpu.VMEM(slot_dual.shape, f32),
            pltpu.VMEM(spend_limit.shape, f32),
            pltpu.VMEM(capacity.shape, f32),
            pltpu.VMEM((LANES, LANES), f32),
            pltpu.VMEM((cap, mask.shape[1], mask.shape[2], LANES), f32),
            pltpu.VMEM((cap, rows, LANES), f32),
            pltpu.VMEM((ITERS + 1, cap, col_lines, LANES), f32),
            pltpu.VMEM((ITERS + 1, cap * row_lines, LANES), f32),
            pltpu.VMEM((cap, rows, LANES), f32),
            pltpu.VMEM((cap, col_lines, LANES), f32),
            pltpu.VMEM((entry, LANES), f32),
            pltpu.VMEM((outer, entry, LANES), f32),
            pltpu.VMEM((outer, entry + 2 * cap, LANES), f32),
            pltpu.VMEM((outer, cap * entry, LANES), f32),
            pltpu.VMEM((outer, cap * entry, LANES), f32),
            pltpu.VMEM((plane, 2 * cap, LANES), f32),
            pltpu.VMEM((plane, cap * entry, LANES), f32),
            pltpu.VMEM((plane, (cap + 1) * entry, LANES), f32),
            pltpu.VMEM((plane, entry, LANES), f32),
            pltpu.VMEM((plane, cap * entry, LANES), f32),
            pltpu.VMEM((plane, (cap + 1) * entry, LANES), f32),
            pltpu.VMEM((plane, entry, LANES), f32),
            pltpu.SemaphoreType.DMA((4, 2, outer)),
            pltpu.SemaphoreType.DMA((4, 2, plane)),
            pltpu.SemaphoreType.DMA((2, cap)),
            pltpu.SemaphoreType.DMA((5,)),
            pltpu.SemaphoreType.DMA((cap,)),
        ],
        compiler_params=pltpu.CompilerParams(
            collective_id=0, has_side_effects=True, vmem_limit_bytes=60 * 1024 * 1024
        ),
    )(tile_adv, tile_slot, mask, adv_dual, slot_dual, spend_limit, capacity, primal_start, cost)
    return pl.pallas_call(
        store,
        out_shape=outs,
        in_specs=[pl.BlockSpec(memory_space=pl.ANY)] * len(outs),
        out_specs=(hbm,) * len(outs),
        scratch_shapes=[pltpu.SemaphoreType.DMA((4 * cap + 2,))],
        compiler_params=pltpu.CompilerParams(vmem_limit_bytes=60 * 1024 * 1024),
    )(*results)


def solution(mesh):
    return jax.shard_map(
        body,
        mesh=mesh,
        in_specs=(
            P("tiles", None, None),
            P("tiles", None, None),
            P("tiles", None, None),
            P("tiles"),
            P("tiles"),
            P("tiles", None),
            P("tiles", None),
            P("tiles", None),
            P("tiles", None),
        ),
        out_specs=(P("tiles", None, None), P("tiles", None), P("tiles", None)),
        check_vma=False,
    )
```

time: 49.6 us -> 163 us (3.29)
  Pallas kernels: 36.7 us -> 162 us
  local copies, waits for them, and re-layouts: 11.8 us -> 0 us
    pallas_call x0 -> x1, Pallas kernels: none -> 128 us  [body(): pl.pallas_call(store, out_shape=outs, in_specs=[pl.BlockSpec(memory_space...]
    unnamed x20 -> x0, local copies, waits for them, and re-layouts: 11.8 us -> none
    pallas_call x1, Pallas kernels: 36.7 us -> 33.5 us  [body(): pl.pallas_call(functools.partial(kernel, outer, inner, cap, rows, cols),...]
where the time goes in v2:
time: 163 us
  Pallas kernels  162 us (99%)
    pallas_call x1, Pallas kernels, body(): pl.pallas_call(store, out_shape=outs, in_specs=[pl.BlockSpec(memory_space...  128 us
    pallas_call x1, Pallas kernels, body(): pl.pallas_call(functools.partial(kernel, outer, inner, cap, rows, cols),...  33.5 us

profile of v2, /device:TPU:0, one launch (start us, length us, event | category | flops | bytes accessed | tf_op | source)
XLA Modules:
  0.0 162.5 jit_solution(3879256918724814866)
XLA Ops:
  0.6 33.5 %shard_map.112 = (f32[2,512,1024]{2,1,0:T(8,128)}, f32[1,512]{1,0:T(1,128)}, f32[1,1024]{1,0:T(1,128)}) custom-call(s32[2]{0:T(128)} %adv_id.1, s32[2]{0:T(128)} %slot_id.1, s32[2,8,64]{2,1,0:T(8,128)} %bitcast.1, f32[1,512]{1,0:T(1,128)} %adv_hbm.1, f32[1,1024]{1,0:T(1,128)} %slot_hbm.1, f32[1,512]{1,0:T(1,128)} %limit_hbm.1, f32[1,1024]{1,0:T(1,128)} %room_hbm.1, ...), custom_call_target="tpu_custom_call" | custom-call | tf_op jit(solution)/shard_map/pallas_call | solution.py:368
  34.1 128.4 %shard_map.113 = (f32[2,512,1024]{2,1,0:T(8,128)}, f32[1,512]{1,0:T(1,128)}, f32[1,1024]{1,0:T(1,128)}) custom-call(f32[2,512,1024]{2,1,0:T(8,128)} %get-tuple-element.6.refs_0_, f32[1,512]{1,0:T(1,128)} %get-tuple-element.7.refs_1_, f32[1,1024]{1,0:T(1,128)} %get-tuple-element.8.refs_2_), custom_call_target="tpu_custom_call" | custom-call | tf_op jit(solution)/shard_map/pallas_call | solution.py:410

commit v3 on v2

--- a/solution.py
+++ b/solution.py
@@ -156,12 +156,18 @@
         zero = jnp.zeros((SUB, LANES), jnp.float32)
         return lax.fori_loop(0, rows // STEP, step, (zero,) * col_lines)
 
-    def keep_sums(slot, t, col):
-        for r in range(row_lines):
-            turned = jnp.transpose(row_part[t, r * LANES:(r + 1) * LANES, :])
-            row_sum[slot, t * row_lines + r:t * row_lines + r + 1, :] = jnp.sum(turned, axis=0, keepdims=True)
+    def keep_cols(slot, t, col):
         for j in range(col_lines):
             col_sum[slot, t, j:j + 1, :] = jnp.sum(col[j], axis=0, keepdims=True)
+
+    def keep_rows(slot):
+        lane = lax.broadcasted_iota(jnp.int32, (LANES, LANES), 1)
+        gathered = jnp.zeros((LANES, LANES), jnp.float32)
+        for t in range(cap):
+            for r in range(row_lines):
+                sums = jnp.sum(row_part[t, r * LANES:(r + 1) * LANES, :], axis=1, keepdims=True)
+                gathered = jnp.where(lane == t * row_lines + r, sums, gathered)
+        row_sum[slot] = jnp.transpose(gathered)[0:cap * row_lines, :]
 
     def prepare(t):
         for made in loads[t]:
@@ -184,7 +190,7 @@
             return tuple(col)
 
         zero = jnp.zeros((SUB, LANES), jnp.float32)
-        keep_sums(0, t, lax.fori_loop(0, rows // STEP, step, (zero,) * col_lines))
+        keep_cols(0, t, lax.fori_loop(0, rows // STEP, step, (zero,) * col_lines))
 
     def less_price(t):
         def step(s, carry):
@@ -196,11 +202,15 @@
 
         lax.fori_loop(0, rows // STEP, step, 0)
 
-    def set_duals(t, adv, slot):
-        for r in range(row_lines):
-            spread = jnp.broadcast_to(0.5 * adv[r:r + 1, :], (LANES, LANES))
-            half_adv[t, r * LANES:(r + 1) * LANES, :] = jnp.transpose(spread)
-        half_slot[t] = 0.5 * slot
+    def set_duals(found):
+        for t, (adv, slot) in enumerate(found):
+            square[t * row_lines:(t + 1) * row_lines, :] = 0.5 * adv
+            half_slot[t] = 0.5 * slot
+        turned = jnp.transpose(square[...])
+        for t in range(cap):
+            for r in range(row_lines):
+                at = t * row_lines + r
+                half_adv[t, r * LANES:(r + 1) * LANES, :] = jnp.broadcast_to(turned[:, at:at + 1], (LANES, LANES))
 
     def update(t, slot):
         slots = [jnp.broadcast_to(half_slot[t, j:j + 1, :], (SUB, LANES)) for j in range(col_lines)]
@@ -212,7 +222,7 @@
             tile[at] = new
             return new
 
-        keep_sums(slot, t, sum_tile(t, value))
+        keep_cols(slot, t, sum_tile(t, value))
 
     def post(buf, slot):
         for t in range(cap):
@@ -277,14 +287,15 @@
     parts(part_start, block_items(dual_buf, 1.0), False, send_start, got_start)
     for t in range(1, cap):
         prepare(t)
+    keep_rows(0)
     rest.arrive()
     part_start.arrive()
 
     old = total(got_start)
-    for t in range(cap):
-        set_duals(t, old[adv_at(cap, t)], old[slot_at(t)])
+    set_duals([(old[adv_at(cap, t)], old[slot_at(t)]) for t in range(cap)])
     for t in range(cap):
         update(t, 1)
+    keep_rows(1)
     post(sums_one, 1)
     send_column(first, sums_one)
     parts(part_one, block_items(rest_buf, -1.0), True, send_one, got_one, go=False)
@@ -296,22 +307,25 @@
     part_one.arrive()
 
     moved = total(got_one)
+    found = []
     for k in range(cap + 1):
         adv, slot = moved[adv_at(cap + 1, k)], moved[slot_at(k)]
         if k < cap:
             adv = jnp.maximum(old[adv_at(cap, k)] + adv / cols, 0.0)
             slot = jnp.maximum(old[slot_at(k)] + slot / rows, 0.0)
-            set_duals(k, adv, slot)
+            found.append((adv, slot))
         else:
             totals[adv_at(1, 0), :] = jnp.maximum(dual_buf[o, adv_at(1, 0), :] + adv / cols, 0.0)
             totals[slot_at(0), :] = jnp.maximum(dual_buf[o, slot_at(0), :] + slot / rows, 0.0)
 
+    set_duals(found)
     stores = []
     for t in range(cap):
         update(t, 2)
         made = pltpu.make_async_copy(tile.at[t], primal_hbm.at[t], out_sems.at[t])
         made.start()
         stores.append(made)
+    keep_rows(2)
     post(sums_two, 2)
     send_column(second, sums_two)
     second.arrive()
@@ -332,19 +346,22 @@
         made.wait()
 
 
-def store(*refs):
-    pieces = refs[-1].shape[0] - 2
-    cap, rows = refs[0].shape[:2]
+def store(primal, adv, slot, primal_out, adv_out, slot_out, held, small, in_sems, out_sems):
+    pieces = in_sems.shape[0] - len(small)
+    cap, rows = primal.shape[:2]
     size = cap * rows // pieces
-    made = []
+    routes = [(adv, small[0], adv_out), (slot, small[1], slot_out)]
     for n in range(pieces):
         at = (n * size // rows, pl.ds(n * size % rows, size))
-        made.append(pltpu.make_async_copy(refs[0].at[at], refs[3].at[at], refs[-1].at[n]))
-    made.append(pltpu.make_async_copy(refs[1], refs[4], refs[-1].at[pieces]))
-    made.append(pltpu.make_async_copy(refs[2], refs[5], refs[-1].at[pieces + 1]))
-    for copy in made:
+        routes.append((primal.at[at], held.at[at], primal_out.at[at]))
+    into = [pltpu.make_async_copy(src, mid, in_sems.at[n]) for n, (src, mid, _) in enumerate(routes)]
+    out = [pltpu.make_async_copy(mid, dst, out_sems.at[n]) for n, (_, mid, dst) in enumerate(routes)]
+    for copy in into:
         copy.start()
-    for copy in made:
+    for first, then in zip(into, out):
+        first.wait()
+        then.start()
+    for copy in out:
         copy.wait()
 
 
@@ -412,7 +429,12 @@
         out_shape=outs,
         in_specs=[pl.BlockSpec(memory_space=pl.ANY)] * len(outs),
         out_specs=(hbm,) * len(outs),
-        scratch_shapes=[pltpu.SemaphoreType.DMA((4 * cap + 2,))],
+        scratch_shapes=[
+            pltpu.VMEM(primal_start.shape, f32),
+            (pltpu.VMEM(adv_dual.shape, f32), pltpu.VMEM(slot_dual.shape, f32)),
+            pltpu.SemaphoreType.DMA((4 * cap + 2,)),
+            pltpu.SemaphoreType.DMA((4 * cap + 2,)),
+        ],
         compiler_params=pltpu.CompilerParams(vmem_limit_bytes=60 * 1024 * 1024),
     )(*results)
 

time: 163 us -> 38.2 us (0.23)
  Pallas kernels: 162 us -> 37.3 us
    pallas_call x1, Pallas kernels: 128 us -> 3.65 us  [body(): pl.pallas_call(store, out_shape=outs, in_specs=[pl.BlockSpec(memory_space...]
where the time goes in v3:
time: 38.2 us; the launch traced here: 37.9 us
  Pallas kernels  37.3 us (98%)
  between operations  0.64 us (2%)
    pallas_call x1, Pallas kernels, body(): pl.pallas_call(functools.partial(kernel, outer, inner, cap, rows, cols),...  33.6 us
    pallas_call x1, Pallas kernels, body(): pl.pallas_call(store, out_shape=outs, in_specs=[pl.BlockSpec(memory_space...  3.65 us

profile of v3, /device:TPU:0, one launch (start us, length us, event | category | flops | bytes accessed | tf_op | source)
XLA Modules:
  0.0 37.9 jit_solution(1915660488284417548)
XLA Ops:
  0.6 33.6 %shard_map.112 = (f32[2,512,1024]{2,1,0:T(8,128)}, f32[1,512]{1,0:T(1,128)}, f32[1,1024]{1,0:T(1,128)}) custom-call(s32[2]{0:T(128)} %adv_id.1, s32[2]{0:T(128)} %slot_id.1, s32[2,8,64]{2,1,0:T(8,128)} %bitcast.1, f32[1,512]{1,0:T(1,128)} %adv_hbm.1, f32[1,1024]{1,0:T(1,128)} %slot_hbm.1, f32[1,512]{1,0:T(1,128)} %limit_hbm.1, f32[1,1024]{1,0:T(1,128)} %room_hbm.1, ...), custom_call_target="tpu_custom_call" | custom-call | tf_op jit(solution)/shard_map/pallas_call | solution.py:385
  34.3 3.7 %shard_map.113 = (f32[2,512,1024]{2,1,0:T(8,128)}, f32[1,512]{1,0:T(1,128)}, f32[1,1024]{1,0:T(1,128)}) custom-call(f32[2,512,1024]{2,1,0:T(8,128)} %get-tuple-element.6.primal, f32[1,512]{1,0:T(1,128)} %get-tuple-element.7.adv, f32[1,1024]{1,0:T(1,128)} %get-tuple-element.8.slot), custom_call_target="tpu_custom_call" | custom-call | tf_op jit(solution)/shard_map/pallas_call | solution.py:427

commit v4 on v3

--- a/solution.py
+++ b/solution.py
@@ -65,6 +65,17 @@
     groups = STEP // SUB
     mask_rows, mask_cols = mask_hbm.shape[2], mask_hbm.shape[1]
 
+    def in_column(k):
+        return lax.rem(o + k, outer) * plane + p
+
+    def in_plane(k):
+        return o * plane + lax.rem(p + k, plane)
+
+    barrier = pltpu.get_barrier_semaphore()
+    peers = [in_column(k) for k in range(1, outer)] + [in_plane(k) for k in range(1, plane)]
+    for peer in peers:
+        pl.semaphore_signal(barrier, inc=1, device_id=(peer,), device_id_type=MESH)
+
     small = [
         pltpu.make_async_copy(src, dst, small_sems.at[n])
         for n, (src, dst) in enumerate((
@@ -82,19 +93,10 @@
             made.start()
         loads.append(pair)
 
-    def in_column(k):
-        return lax.rem(o + k, outer) * plane + p
-
-    def in_plane(k):
-        return o * plane + lax.rem(p + k, plane)
-
-    barrier = pltpu.get_barrier_semaphore()
-    peers = [in_column(k) for k in range(1, outer)] + [in_plane(k) for k in range(1, plane)]
-    for peer in peers:
-        pl.semaphore_signal(barrier, inc=1, device_id=(peer,), device_id_type=MESH)
-
-    exchanges = [Copies(column_sems.at[g]) for g in range(4)] + [Copies(plane_sems.at[g]) for g in range(4)]
-    duals, rest, first, second, named, part_start, part_one, part_two = exchanges
+    along = [Copies(column_sems.at[g]) for g in range(2 + 2 * cap)]
+    across = [Copies(plane_sems.at[g]) for g in range(4)]
+    duals, rest, first, second = along[0], along[1], along[2:2 + cap], along[2 + cap:]
+    named, part_start, part_one, part_two = across
 
     def slot_at(e):
         return slice(e * col_lines, (e + 1) * col_lines)
@@ -160,14 +162,13 @@
         for j in range(col_lines):
             col_sum[slot, t, j:j + 1, :] = jnp.sum(col[j], axis=0, keepdims=True)
 
-    def keep_rows(slot):
+    def keep_rows(slot, t):
         lane = lax.broadcasted_iota(jnp.int32, (LANES, LANES), 1)
         gathered = jnp.zeros((LANES, LANES), jnp.float32)
-        for t in range(cap):
-            for r in range(row_lines):
-                sums = jnp.sum(row_part[t, r * LANES:(r + 1) * LANES, :], axis=1, keepdims=True)
-                gathered = jnp.where(lane == t * row_lines + r, sums, gathered)
-        row_sum[slot] = jnp.transpose(gathered)[0:cap * row_lines, :]
+        for r in range(row_lines):
+            sums = jnp.sum(row_part[t, r * LANES:(r + 1) * LANES, :], axis=1, keepdims=True)
+            gathered = jnp.where(lane == r, sums, gathered)
+        row_sum[slot, t] = jnp.transpose(gathered)[0:row_lines, :]
 
     def prepare(t):
         for made in loads[t]:
@@ -224,22 +225,20 @@
 
         keep_cols(slot, t, sum_tile(t, value))
 
-    def post(buf, slot):
-        for t in range(cap):
-            at = slice(t * row_lines, (t + 1) * row_lines)
-            buf[o, slot_at(t), :] = 2.0 * col_sum[slot, t] - col_sum[slot - 1, t]
-            buf[o, adv_at(cap, t), :] = 2.0 * row_sum[slot, at, :] - row_sum[slot - 1, at, :]
+    def post(buf, slot, t):
+        buf[t, o, slot_at(0), :] = 2.0 * col_sum[slot, t] - col_sum[slot - 1, t]
+        buf[t, o, adv_at(1, 0), :] = 2.0 * row_sum[slot, t] - row_sum[slot - 1, t]
 
     def splat(value):
         return jnp.full((1, LANES), value.astype(jnp.float32))
 
-    def tile_items(buf):
+    def tile_items(buf, t):
         return [
             (
                 rest_buf[b, id_line + t:id_line + t + 1, :], rest_buf[b, id_line + cap + t:id_line + cap + t + 1, :],
-                buf[b, adv_at(cap, t), :], buf[b, slot_at(t), :],
+                buf[t, b, adv_at(1, 0), :], buf[t, b, slot_at(0), :],
             )
-            for b in range(outer) for t in range(cap)
+            for b in range(outer)
         ]
 
     def block_items(buf, sign):
@@ -281,13 +280,12 @@
             value = value + got[k]
         return value
 
-    prepare(0)
     named.arrive()
     duals.arrive()
     parts(part_start, block_items(dual_buf, 1.0), False, send_start, got_start)
-    for t in range(1, cap):
+    for t in range(cap):
         prepare(t)
-    keep_rows(0)
+        keep_rows(0, t)
     rest.arrive()
     part_start.arrive()
 
@@ -295,13 +293,14 @@
     set_duals([(old[adv_at(cap, t)], old[slot_at(t)]) for t in range(cap)])
     for t in range(cap):
         update(t, 1)
-    keep_rows(1)
-    post(sums_one, 1)
-    send_column(first, sums_one)
+        keep_rows(1, t)
+        post(sums_one, 1, t)
+        send_column(first[t], sums_one.at[t])
     parts(part_one, block_items(rest_buf, -1.0), True, send_one, got_one, go=False)
     less_price(0)
-    first.arrive()
-    parts(part_one, tile_items(sums_one), True, send_one, got_one, add=True)
+    for t in range(cap):
+        first[t].arrive()
+        parts(part_one, tile_items(sums_one, t), True, send_one, got_one, add=True, go=t == cap - 1)
     for t in range(1, cap):
         less_price(t)
     part_one.arrive()
@@ -325,11 +324,12 @@
         made = pltpu.make_async_copy(tile.at[t], primal_hbm.at[t], out_sems.at[t])
         made.start()
         stores.append(made)
-    keep_rows(2)
-    post(sums_two, 2)
-    send_column(second, sums_two)
-    second.arrive()
-    parts(part_two, tile_items(sums_two), "alone", send_two, got_two)
+        keep_rows(2, t)
+        post(sums_two, 2, t)
+        send_column(second[t], sums_two.at[t])
+    for t in range(cap):
+        second[t].arrive()
+        parts(part_two, tile_items(sums_two, t), "alone", send_two, got_two, add=t > 0, go=t == cap - 1)
     part_two.arrive()
 
     use = total(got_two)
@@ -340,7 +340,7 @@
     for r in range(col_lines):
         slot_out[0:1, r * LANES:(r + 1) * LANES] = jnp.maximum(slot[r:r + 1, :], 0.0)
 
-    for copies in exchanges:
+    for copies in along + across:
         copies.drain()
     for made in stores:
         made.wait()
@@ -399,14 +399,14 @@
             pltpu.VMEM((cap, mask.shape[1], mask.shape[2], LANES), f32),
             pltpu.VMEM((cap, rows, LANES), f32),
             pltpu.VMEM((ITERS + 1, cap, col_lines, LANES), f32),
-            pltpu.VMEM((ITERS + 1, cap * row_lines, LANES), f32),
+            pltpu.VMEM((ITERS + 1, cap, row_lines, LANES), f32),
             pltpu.VMEM((cap, rows, LANES), f32),
             pltpu.VMEM((cap, col_lines, LANES), f32),
             pltpu.VMEM((entry, LANES), f32),
             pltpu.VMEM((outer, entry, LANES), f32),
             pltpu.VMEM((outer, entry + 2 * cap, LANES), f32),
-            pltpu.VMEM((outer, cap * entry, LANES), f32),
-            pltpu.VMEM((outer, cap * entry, LANES), f32),
+            pltpu.VMEM((cap, outer, entry, LANES), f32),
+            pltpu.VMEM((cap, outer, entry, LANES), f32),
             pltpu.VMEM((plane, 2 * cap, LANES), f32),
             pltpu.VMEM((plane, cap * entry, LANES), f32),
             pltpu.VMEM((plane, (cap + 1) * entry, LANES), f32),
@@ -414,7 +414,7 @@
             pltpu.VMEM((plane, cap * entry, LANES), f32),
             pltpu.VMEM((plane, (cap + 1) * entry, LANES), f32),
             pltpu.VMEM((plane, entry, LANES), f32),
-            pltpu.SemaphoreType.DMA((4, 2, outer)),
+            pltpu.SemaphoreType.DMA((2 + 2 * cap, 2, outer)),
             pltpu.SemaphoreType.DMA((4, 2, plane)),
             pltpu.SemaphoreType.DMA((2, cap)),
             pltpu.SemaphoreType.DMA((5,)),

time: 38.2 us -> 38.4 us (level)
  no operation moved by 1% of the time
where the time goes in v4:
time: 38.4 us; the launch traced here: 38.2 us
  Pallas kernels  37.5 us (98%)
  between operations  0.64 us (2%)
    pallas_call x1, Pallas kernels, body(): pl.pallas_call(functools.partial(kernel, outer, inner, cap, rows, cols),...  33.9 us
    pallas_call x1, Pallas kernels, body(): pl.pallas_call(store, out_shape=outs, in_specs=[pl.BlockSpec(memory_space...  3.65 us

profile of v4, /device:TPU:0, one launch (start us, length us, event | category | flops | bytes accessed | tf_op | source)
XLA Modules:
  0.0 38.2 jit_solution(11318971174137026679)
XLA Ops:
  0.6 33.9 %shard_map.112 = (f32[2,512,1024]{2,1,0:T(8,128)}, f32[1,512]{1,0:T(1,128)}, f32[1,1024]{1,0:T(1,128)}) custom-call(s32[2]{0:T(128)} %adv_id.1, s32[2]{0:T(128)} %slot_id.1, s32[2,8,64]{2,1,0:T(8,128)} %bitcast.1, f32[1,512]{1,0:T(1,128)} %adv_hbm.1, f32[1,1024]{1,0:T(1,128)} %slot_hbm.1, f32[1,512]{1,0:T(1,128)} %limit_hbm.1, f32[1,1024]{1,0:T(1,128)} %room_hbm.1, ...), custom_call_target="tpu_custom_call" | custom-call | tf_op jit(solution)/shard_map/pallas_call | solution.py:385
  34.5 3.7 %shard_map.113 = (f32[2,512,1024]{2,1,0:T(8,128)}, f32[1,512]{1,0:T(1,128)}, f32[1,1024]{1,0:T(1,128)}) custom-call(f32[2,512,1024]{2,1,0:T(8,128)} %get-tuple-element.6.primal, f32[1,512]{1,0:T(1,128)} %get-tuple-element.7.adv, f32[1,1024]{1,0:T(1,128)} %get-tuple-element.8.slot), custom_call_target="tpu_custom_call" | custom-call | tf_op jit(solution)/shard_map/pallas_call | solution.py:427

commit v5 on v3

--- a/solution.py
+++ b/solution.py
@@ -10,7 +10,7 @@
 ITERS = 2
 LANES = 128
 SUB = 8
-STEP = 32
+STEP = 64
 MESH = pl.DeviceIdType.MESH
 
 
@@ -230,6 +230,9 @@
             buf[o, slot_at(t), :] = 2.0 * col_sum[slot, t] - col_sum[slot - 1, t]
             buf[o, adv_at(cap, t), :] = 2.0 * row_sum[slot, at, :] - row_sum[slot - 1, at, :]
 
+    def wide(line, lines):
+        return jnp.broadcast_to(line, (lines, LANES))
+
     def splat(value):
         return jnp.full((1, LANES), value.astype(jnp.float32))
 
@@ -262,8 +265,8 @@
             adv = into[adv_at(n, e), :] if add else jnp.zeros((row_lines, LANES), jnp.float32)
             slot = into[slot_at(e), :] if add else jnp.zeros((col_lines, LANES), jnp.float32)
             for a_of, b_of, by_row, by_col in items:
-                adv = adv + jnp.where(a_of == a, 1.0, 0.0) * by_row
-                slot = slot + jnp.where(b_of == b, 1.0, 0.0) * by_col
+                adv = adv + jnp.where(wide(a_of, row_lines) == wide(a, row_lines), by_row, 0.0)
+                slot = slot + jnp.where(wide(b_of, col_lines) == wide(b, col_lines), by_col, 0.0)
             into[adv_at(n, e), :] = adv
             into[slot_at(e), :] = slot
 
@@ -281,11 +284,10 @@
             value = value + got[k]
         return value
 
-    prepare(0)
     named.arrive()
     duals.arrive()
     parts(part_start, block_items(dual_buf, 1.0), False, send_start, got_start)
-    for t in range(1, cap):
+    for t in range(cap):
         prepare(t)
     keep_rows(0)
     rest.arrive()

time: 38.2 us -> 38.1 us (level)
  no operation moved by 1% of the time
where the time goes in v5:
time: 38.1 us; the launch traced here: 37.9 us
  Pallas kernels  37.3 us (98%)
  between operations  0.64 us (2%)
    pallas_call x1, Pallas kernels, body(): pl.pallas_call(functools.partial(kernel, outer, inner, cap, rows, cols),...  33.6 us
    pallas_call x1, Pallas kernels, body(): pl.pallas_call(store, out_shape=outs, in_specs=[pl.BlockSpec(memory_space...  3.65 us

profile of v5, /device:TPU:0, one launch (start us, length us, event | category | flops | bytes accessed | tf_op | source)
XLA Modules:
  0.0 37.9 jit_solution(16240772522522036394)
XLA Ops:
  0.6 33.6 %shard_map.112 = (f32[2,512,1024]{2,1,0:T(8,128)}, f32[1,512]{1,0:T(1,128)}, f32[1,1024]{1,0:T(1,128)}) custom-call(s32[2]{0:T(128)} %adv_id.1, s32[2]{0:T(128)} %slot_id.1, s32[2,8,64]{2,1,0:T(8,128)} %bitcast.1, f32[1,512]{1,0:T(1,128)} %adv_hbm.1, f32[1,1024]{1,0:T(1,128)} %slot_hbm.1, f32[1,512]{1,0:T(1,128)} %limit_hbm.1, f32[1,1024]{1,0:T(1,128)} %room_hbm.1, ...), custom_call_target="tpu_custom_call" | custom-call | tf_op jit(solution)/shard_map/pallas_call | solution.py:387
  34.3 3.7 %shard_map.113 = (f32[2,512,1024]{2,1,0:T(8,128)}, f32[1,512]{1,0:T(1,128)}, f32[1,1024]{1,0:T(1,128)}) custom-call(f32[2,512,1024]{2,1,0:T(8,128)} %get-tuple-element.6.primal, f32[1,512]{1,0:T(1,128)} %get-tuple-element.7.adv, f32[1,1024]{1,0:T(1,128)} %get-tuple-element.8.slot), custom_call_target="tpu_custom_call" | custom-call | tf_op jit(solution)/shard_map/pallas_call | solution.py:429
